TPU v7x, 32 devices: a whole 2x2x4 slice. The times are simulated.
32 devices in a mesh: dp: 4 (over x, core), gx: 2 (over y), gy: 4 (over z).
Axes of the slice: x: 2, y: 2, z: 4, core: 2. Of those that a mesh axis runs over, the one named last changes fastest.
Arguments:
- hidden_in: bfloat16 [16384, 1024], P(('dp', 'gx'), 'gy'), may hold values from -15 to 15
- ln1_gain: float32 [1024], P('gy'), may hold values from 0.3 to 2
- ln1_bias: float32 [1024], P('gy'), may hold values from -3 to 3
- ln2_gain: float32 [1024], P('gy'), may hold values from 0.3 to 2
- ln2_bias: float32 [1024], P('gy'), may hold values from -3 to 3
- w_qkv: bfloat16 [1024, 3072], P('gy', 'gx'), may hold values from -0.1875 to 0.1875
- b_qkv: float32 [3072], P('gx'), may hold values from -3 to 3
- w_dense: bfloat16 [1024, 1024], P('gx', 'gy'), may hold values from -1 to 1
- b_dense: float32 [1024], P('gy'), may hold values from -3 to 3
- w_up: bfloat16 [1024, 4096], P('gy', 'gx'), may hold values from -0.1875 to 0.1875
- b_up: float32 [4096], P('gx'), may hold values from -3 to 3
- w_down: bfloat16 [4096, 1024], P('gx', 'gy'), may hold values from -0.09375 to 0.09375
- b_down: float32 [1024], P('gy'), may hold values from -3 to 3
- cotangent: bfloat16 [16384, 1024], P(('dp', 'gx'), 'gy'), may hold values from -6 to 6
Outputs:
- hidden_out: bfloat16 [16384, 1024], P(('dp', 'gx'), 'gy')
- grad_input: bfloat16 [16384, 1024], P(('dp', 'gx'), 'gy')
- grad_ln1_gain: float32 [1024], P('gy')
- grad_ln1_bias: float32 [1024], P('gy')
- grad_ln2_gain: float32 [1024], P('gy')
- grad_ln2_bias: float32 [1024], P('gy')
- grad_w_qkv: float32 [1024, 3072], P('gy', 'gx')
- grad_b_qkv: float32 [3072], P('gx')
- grad_w_dense: float32 [1024, 1024], P('gx', 'gy')
- grad_b_dense: float32 [1024], P('gy')
- grad_w_up: float32 [1024, 4096], P('gy', 'gx')
- grad_b_up: float32 [4096], P('gx')
- grad_w_down: float32 [4096, 1024], P('gx', 'gy')
- grad_b_down: float32 [1024], P('gy')
All inputs are finite; a program needn't handle non-finite values.
Results may differ from a plain program's by a relative error of at most 0.012.
The roundings to bfloat16 on the way count: a program that leaves them out, or rounds other values in their place, can miss the bound.
Values may be sent and summed in bfloat16 or wider, within the bound.
No kernel may reach another device: no remote copies, remote signals or barrier semaphores. Data moves between devices by JAX's collectives and lax.ppermute only.
A program may use at most 256 MiB of HBM per device.

v0:
```python
import jax
import jax.numpy as jnp
from jax import lax
from jax.sharding import PartitionSpec as P

D = 1024
HD = 64
ROT = 16
LEN = 1024


eps_norm = 1e-05


def leading(left, right):
    return lax.dot_general(
        left, right, (((0,), (0,)), ((), ())), preferred_element_type=jnp.float32
    )


def trailing(left, right):
    return lax.dot_general(
        left, right, (((1,), (1,)), ((), ())), preferred_element_type=jnp.float32
    )


def angles(token_count):
    places = (jnp.arange(token_count) % LEN).astype(jnp.float32)
    freqs = 10000.0 ** (-jnp.arange(ROT // 2).astype(jnp.float32) * 2.0 / ROT)
    turned = places[:, None] * freqs[None, :]
    return (jnp.cos(turned)[:, None, :], jnp.sin(turned)[:, None, :])


def rotate(vectors, cosine, sine_part):
    half_rot = ROT // 2
    first_half = vectors[..., :half_rot]
    second_half = vectors[..., half_rot:ROT]
    return jnp.concatenate(
        [
            first_half * cosine - second_half * sine_part,
            second_half * cosine + first_half * sine_part,
            vectors[..., ROT:],
        ],
        axis=-1,
    )


def gelu_exact(values_in):
    return jax.nn.gelu(values_in, approximate=False)


def local(
    hidden_in,
    ln1_gain,
    ln1_bias,
    ln2_gain,
    ln2_bias,
    w_qkv,
    b_qkv,
    w_dense,
    b_dense,
    w_up,
    b_up,
    w_down,
    b_down,
    cotangent,
):
    inputs = hidden_in.astype(jnp.float32)
    row_total, row_square = lax.psum(
        (jnp.sum(inputs, axis=1), jnp.sum(inputs * inputs, axis=1)), "gy"
    )
    row_mean = row_total / D
    inv_std = lax.rsqrt(row_square / D - row_mean * row_mean + eps_norm)[:, None]
    normed = (inputs - row_mean[:, None]) * inv_std
    attn_in = (normed * ln1_gain + ln1_bias).astype(jnp.bfloat16)
    mlp_in = (normed * ln2_gain + ln2_bias).astype(jnp.bfloat16)
    attn_rows, mlp_rows = (
        lax.all_gather(attn_in, "gx", axis=0, tiled=True),
        lax.all_gather(mlp_in, "gx", axis=0, tiled=True),
    )
    projected, pre_act = (
        lax.psum_scatter(
            jnp.dot(attn_rows, w_qkv, preferred_element_type=jnp.float32),
            "gy",
            scatter_dimension=0,
            tiled=True,
        ),
        lax.psum_scatter(
            jnp.dot(mlp_rows, w_up, preferred_element_type=jnp.float32),
            "gy",
            scatter_dimension=0,
            tiled=True,
        ),
    )
    projected = projected + b_qkv
    pre_act = pre_act + b_up
    own_rows = projected.shape[0]
    local_heads = projected.shape[1] // (3 * HD)
    triple = projected.reshape(own_rows, local_heads, 3, HD)
    cosine, sine_part = angles(own_rows)
    seq_count = own_rows // LEN
    block_rows = min(512, LEN)
    per_seq = LEN // block_rows
    item_count = seq_count * per_seq
    score_scale = HD ** (-0.5)
    shape_four = (seq_count, LEN, local_heads, HD)
    query_four = rotate(triple[:, :, 0], cosine, sine_part).astype(jnp.bfloat16).reshape(shape_four)
    key_four = rotate(triple[:, :, 1], cosine, sine_part).astype(jnp.bfloat16).reshape(shape_four)
    value_four = triple[:, :, 2].astype(jnp.bfloat16).reshape(shape_four)

    def block_of(tensor_four, seq_index, start_row):
        whole_seq = lax.dynamic_index_in_dim(tensor_four, seq_index, 0, keepdims=False)
        return lax.dynamic_slice_in_dim(whole_seq, start_row, block_rows, 0)

    def scores_of(item_index):
        seq_index = item_index // per_seq
        start_row = item_index % per_seq * block_rows
        query_block = block_of(query_four, seq_index, start_row)
        key_seq = lax.dynamic_index_in_dim(key_four, seq_index, 0, keepdims=False)
        value_seq = lax.dynamic_index_in_dim(value_four, seq_index, 0, keepdims=False)
        raw_scores = (
            jnp.einsum("qhe,khe->hqk", query_block, key_seq, preferred_element_type=jnp.float32)
            * score_scale
        )
        causal = (start_row + jnp.arange(block_rows))[:, None] >= jnp.arange(LEN)[None, :]
        masked = jnp.where(causal[None], raw_scores, -1e30)
        return (masked, query_block, key_seq, value_seq, seq_index, start_row)

    def forward_item(item_index):
        masked, query_block, key_seq, value_seq, seq_index, start_row = scores_of(item_index)
        row_top = jnp.max(masked, axis=-1, keepdims=True)
        exponent = jnp.exp(masked - row_top)
        row_sums = jnp.sum(exponent, axis=-1, keepdims=True)
        weights = (exponent / row_sums).astype(jnp.bfloat16)
        mixed_block = jnp.einsum(
            "hqk,khe->qhe", weights, value_seq, preferred_element_type=jnp.float32
        )
        return (mixed_block, (row_top + jnp.log(row_sums))[..., 0])

    mixed, log_rows = lax.map(forward_item, jnp.arange(item_count))
    heads_low = mixed.reshape(own_rows, local_heads * HD).astype(jnp.bfloat16)
    act_low = gelu_exact(pre_act).astype(jnp.bfloat16)
    heads_rows, act_rows = (
        lax.all_gather(heads_low, "gy", axis=0, tiled=True),
        lax.all_gather(act_low, "gy", axis=0, tiled=True),
    )
    branch_terms = jnp.dot(heads_rows, w_dense, preferred_element_type=jnp.float32) + jnp.dot(
        act_rows, w_down, preferred_element_type=jnp.float32
    )
    branch_total = lax.psum_scatter(branch_terms, "gx", scatter_dimension=0, tiled=True)
    hidden_out = (inputs + branch_total + b_dense + b_down).astype(jnp.bfloat16)
    grad_rows = lax.all_gather(cotangent, "gx", axis=0, tiled=True)
    grad_b_out = jnp.sum(grad_rows.astype(jnp.float32), axis=0)
    grad_w_dense = leading(heads_rows, grad_rows)
    grad_w_down = leading(act_rows, grad_rows)
    grad_heads, grad_act = (
        lax.psum_scatter(trailing(grad_rows, w_dense), "gy", scatter_dimension=0, tiled=True),
        lax.psum_scatter(trailing(grad_rows, w_down), "gy", scatter_dimension=0, tiled=True),
    )
    grad_pre = jax.vjp(gelu_exact, pre_act)[1](grad_act)[0].astype(jnp.bfloat16)
    grad_mixed = grad_heads.astype(jnp.bfloat16).reshape(shape_four)

    def backward_item(packed):
        item_index, log_block = packed
        masked, query_block, key_seq, value_seq, seq_index, start_row = scores_of(item_index)
        grad_block = block_of(grad_mixed, seq_index, start_row)
        weights = jnp.exp(masked - log_block[..., None])
        grad_weights = jnp.einsum(
            "qhe,khe->hqk", grad_block, value_seq, preferred_element_type=jnp.float32
        )
        row_inner = jnp.sum(weights * grad_weights, axis=-1, keepdims=True)
        grad_scores = (weights * (grad_weights - row_inner)).astype(jnp.bfloat16)
        grad_query = (
            jnp.einsum("hqk,khe->qhe", grad_scores, key_seq, preferred_element_type=jnp.float32)
            * score_scale
        )
        grad_key = (
            jnp.einsum("hqk,qhe->khe", grad_scores, query_block, preferred_element_type=jnp.float32)
            * score_scale
        )
        grad_value = jnp.einsum(
            "hqk,qhe->khe",
            weights.astype(jnp.bfloat16),
            grad_block,
            preferred_element_type=jnp.float32,
        )
        return (grad_query, grad_key, grad_value)

    grad_query, grad_key, grad_value = lax.map(backward_item, (jnp.arange(item_count), log_rows))
    grad_query = grad_query.reshape(own_rows, local_heads, HD)
    grad_key = (
        grad_key.reshape(seq_count, per_seq, LEN, local_heads, HD)
        .sum(axis=1)
        .reshape(own_rows, local_heads, HD)
    )
    grad_value = (
        grad_value.reshape(seq_count, per_seq, LEN, local_heads, HD)
        .sum(axis=1)
        .reshape(own_rows, local_heads, HD)
    )
    grad_qkv = (
        jnp.stack(
            [
                rotate(grad_query, cosine, -sine_part),
                rotate(grad_key, cosine, -sine_part),
                grad_value,
            ],
            axis=2,
        )
        .reshape(own_rows, local_heads * 3 * HD)
        .astype(jnp.bfloat16)
    )
    qkv_rows, pre_rows = (
        lax.all_gather(grad_qkv, "gy", axis=0, tiled=True),
        lax.all_gather(grad_pre, "gy", axis=0, tiled=True),
    )
    grad_b_qkv = jnp.sum(qkv_rows.astype(jnp.float32), axis=0)
    grad_b_up = jnp.sum(pre_rows.astype(jnp.float32), axis=0)
    grad_w_qkv = leading(attn_rows, qkv_rows)
    grad_w_up = leading(mlp_rows, pre_rows)
    grad_attn, grad_mlp = (
        lax.psum_scatter(trailing(qkv_rows, w_qkv), "gx", scatter_dimension=0, tiled=True),
        lax.psum_scatter(trailing(pre_rows, w_up), "gx", scatter_dimension=0, tiled=True),
    )
    grad_normed = grad_attn * ln1_gain + grad_mlp * ln2_gain
    grad_total, grad_cross = lax.psum(
        (jnp.sum(grad_normed, axis=1), jnp.sum(grad_normed * normed, axis=1)), "gy"
    )
    grad_input = (
        cotangent.astype(jnp.float32)
        + inv_std * (grad_normed - grad_total[:, None] / D - normed * grad_cross[:, None] / D)
    ).astype(jnp.bfloat16)
    norm_sums = lax.psum(
        (
            jnp.sum(grad_attn * normed, axis=0),
            jnp.sum(grad_attn, axis=0),
            jnp.sum(grad_mlp * normed, axis=0),
            jnp.sum(grad_mlp, axis=0),
        ),
        ("dp", "gx"),
    )
    weight_sums = lax.psum(
        (grad_w_qkv, grad_b_qkv, grad_w_dense, grad_b_out, grad_w_up, grad_b_up, grad_w_down), "dp"
    )
    return (
        hidden_out,
        grad_input,
        norm_sums[0],
        norm_sums[1],
        norm_sums[2],
        norm_sums[3],
        weight_sums[0],
        weight_sums[1],
        weight_sums[2],
        weight_sums[3],
        weight_sums[4],
        weight_sums[5],
        weight_sums[6],
        weight_sums[3],
    )


def solution(mesh):
    placed = (
        P(("dp", "gx"), "gy"),
        P("gy"),
        P("gy"),
        P("gy"),
        P("gy"),
        P("gy", "gx"),
        P("gx"),
        P("gx", "gy"),
        P("gy"),
        P("gy", "gx"),
        P("gx"),
        P("gx", "gy"),
        P("gy"),
        P(("dp", "gx"), "gy"),
    )
    return jax.shard_map(
        local,
        mesh=mesh,
        in_specs=placed,
        out_specs=(
            P(("dp", "gx"), "gy"),
            P(("dp", "gx"), "gy"),
            P("gy"),
            P("gy"),
            P("gy"),
            P("gy"),
            P("gy", "gx"),
            P("gx"),
            P("gx", "gy"),
            P("gy"),
            P("gy", "gx"),
            P("gx"),
            P("gx", "gy"),
            P("gy"),
        ),
        check_vma=False,
    )
```

profile of v0, /device:TPU:0, one launch (start us, length us, event | category | flops | bytes accessed | tf_op | source)
XLA Modules:
  0.0 2975.2 jit_solution(3633931358253806583)
XLA Ops:
  9.8 20.5 all-reduce.2
  34.5 10.9 all-gather.16.cloned.1.call-done
  51.6 29.1 all-gather.8.cloned.1.call-done
  80.7 12.4 fusion.79
  93.2 22.8 all-gather.12.cloned.1.call-done
  116.0 15.3 fusion.80
  132.9 13.4 fusion.84
  147.4 115.3 %reduce-scatter.14.cloned.1.call-done = f32[1024,512]{1,0:T(8,128)} async-done(((f32[4096,512]{1,0:T(8,128)}), f32[1024,512]{1,0:T(8,128)}) %reduce-scatter.14.cloned.1.call-update) | async-done | bytes 2097168 | tf_op jit(solution)/shard_map/reduce_scatter | solution.py:157
  265.7 414.3 %reduce-scatter.8.cloned.1.call-done = f32[1024,1536]{1,0:T(8,128)} async-done(((f32[4096,1536]{1,0:T(8,128)}), f32[1024,1536]{1,0:T(8,128)}) %reduce-scatter.8.cloned.1.call-update) | async-done | bytes 6291472 | tf_op jit(solution)/shard_map/reduce_scatter | solution.py:82
  700.1 34.4 %while.30 = (s32[]{:T(128)}, bf16[2,512,8,64]{1,3,2,0:T(8,128)(2,1)S(1)}, f32[2,8,512]{2,1,0:T(8,128)S(1)}, s32[2]{0:T(128)S(1)}, bf16[1,1024,8,64]{1,3,2,0:T(8,...) while((s32[]{:T(128)}, ...), condition=%wide.region_8.9_spmd, body=%wide.region_5.8_spmd.sunk | while | flops 1124594176 | bytes 56234292 | solution.py:140
  735.5 134.4 %while.31 = (s32[]{:T(128)}, f32[2,512,8,64]{1,0,3,2:T(2,128)}, f32[2,1024,8,64]{1,3,2,0:T(8,128)}, f32[2,1024,8,64]{1,3,2,0:T(8,128)}, s32[2]{0:T(128)S(1)}, /*...) while((s32[]{:T(128)}, f32[2,512,8,64]{1,0,3,2:T(2,128)}, ...), condition=%wide.region_14.15_spmd, body=%wide.region_12.14_spmd.sunk | while | flops 2723410432 | bytes 221598288 | solution.py:189
  743.9 12.0 multiply_reduce_fusion.2
  782.8 19.6 dynamic_update_slice.46
  810.6 12.0 multiply_reduce_fusion.2
  849.9 19.6 dynamic_update_slice.46
  889.5 346.8 %reduce-scatter.10.cloned.1.call-done = f32[1024,2048]{1,0:T(8,128)} async-done(((f32[4096,2048]{1,0:T(8,128)}), f32[1024,2048]{1,0:T(8,128)}) %reduce-scatter.10.cloned.1.call-update) | async-done | bytes 8388624 | tf_op jit(solution)/shard_map/reduce_scatter | solution.py:88
  1236.3 555.2 %reduce-scatter.18.cloned.1.call-done = f32[1024,2048]{1,0:T(8,128)} async-done(((f32[4096,2048]{1,0:T(8,128)}), f32[1024,2048]{1,0:T(8,128)}) %reduce-scatter.18.cloned.1.call-update) | async-done | bytes 8388624 | tf_op jit(solution)/shard_map/reduce_scatter | solution.py:158
  1791.4 23.2 add_convert_fusion
  1828.1 183.9 %all-gather.18.cloned.1.call-done = bf16[4096,1536]{0,1:T(8,128)(2,1)} async-done(((bf16[1024,1536]{0,1:T(8,128)(2,1)}), bf16[4096,1536]{0,1:T(8,128)(2,1)}) %all-gather.18.cloned.1.call-update) | async-done | bytes 12582928 | tf_op jit(solution)/shard_map/all_gather | solution.py:214
  2012.0 10.5 fusion.83
  2022.6 276.1 %all-gather.14.cloned.1.call-done = bf16[4096,2048]{1,0:T(8,128)(2,1)} async-done(((bf16[1024,2048]{1,0:T(8,128)(2,1)}), bf16[4096,2048]{1,0:T(8,128)(2,1)}) %all-gather.14.cloned.1.call-update) | async-done | bytes 16777232 | tf_op jit(solution)/shard_map/all_gather | solution.py:145
  2308.8 71.0 %all-gather.10.cloned.1.call-done = bf16[4096,512]{0,1:T(8,128)(2,1)} async-done(((bf16[1024,512]{0,1:T(8,128)(2,1)}), bf16[4096,512]{0,1:T(8,128)(2,1)}) %all-gather.10.cloned.1.call-update) | async-done | bytes 4194320 | tf_op jit(solution)/shard_map/all_gather | solution.py:144
  2386.8 280.0 %all-gather.20.cloned.1.call-done = bf16[4096,2048]{1,0:T(8,128)(2,1)} async-done(((bf16[1024,2048]{1,0:T(8,128)(2,1)}), bf16[4096,2048]{1,0:T(8,128)(2,1)}) %all-gather.20.cloned.1.call-update) | async-done | bytes 16777232 | tf_op jit(solution)/shard_map/all_gather | solution.py:215
  2666.7 12.6 fusion.85
  2683.6 10.2 fusion.86
  2693.9 10.3 fusion.89
  2724.5 12.4 all-reduce.3
  2736.9 41.3 %reduce-scatter.12.cloned.1.call-done = f32[2048,256]{1,0:T(8,128)} async-done(((f32[4096,256]{1,0:T(8,128)}), f32[2048,256]{1,0:T(8,128)}) %reduce-scatter.12.cloned.1.call-update) | async-done | bytes 2097168 | tf_op jit(solution)/shard_map/reduce_scatter | solution.py:150
  2778.1 56.6 %reduce-scatter.20.cloned.1.call-done = f32[2048,256]{1,0:T(8,128)} async-done(((f32[4096,256]{1,0:T(8,128)}), f32[2048,256]{1,0:T(8,128)}) %reduce-scatter.20.cloned.1.call-update) | async-done | bytes 2097168 | tf_op jit(solution)/shard_map/reduce_scatter | solution.py:223
  2839.6 13.4 all-reduce
  2853.0 18.7 all-reduce.1
  2875.9 82.7 %all-reduce.7.cloned.1.call-done = (f32[256,1536]{1,0:T(8,128)}, f32[512,256]{1,0:T(8,128)}, f32[256,2048]{1,0:T(8,128)}, f32[2048,256]{1,0:T(8,128)}) async-done(((f32[256,1536]{1,0:T(8,128)}, f32[512,256]{1,0:T(8,128)}, f32[256,2048]{1,0:T(8,128)}, f32[2048,256]{1,0:T(8,128)}), (f32[256,1536]{1,0:T(8,128)}, f32[512,256]{1,0:T(8,128)}, f32[256,2048]{1,0:T(8,128)}, ...) | async-done | bytes 6291472 | tf_op jit(solution)/shard_map/psum | solution.py:242
  (212 shorter events, 229.9 us)
Async XLA Ops:
  7.2 124.2 %copy-start = (bf16[2048,256]{1,0:T(8,128)(2,1)S(1)}, bf16[2048,256]{1,0:T(8,128)(2,1)}, u32[]{:S(2)}) copy-start(bf16[2048,256]{1,0:T(8,128)(2,1)} %param.29) | copy-start | bytes 3145732
  7.2 38.2 %all-gather.16.cloned.1.call-start = ((), (), s32[]{:S(2)}) async-start(), calls=%async_computation.14 | async-start | bytes 3145728 | tf_op jit(solution)/shard_map/all_gather | solution.py:152
  7.9 72.8 %all-gather.8.cloned.1.call-start = ((), (), s32[]{:S(2)}) async-start(), calls=%async_computation.7 | async-start | bytes 3145728 | tf_op jit(solution)/shard_map/all_gather | solution.py:78
  33.7 82.3 %all-gather.12.cloned.1.call-start = ((), (), s32[]{:S(2)}) async-start(), calls=%async_computation.10 | async-start | bytes 3145728 | tf_op jit(solution)/shard_map/all_gather | solution.py:79
  34.4 46.3 %copy-start.17 = (bf16[256,1536]{1,0:T(8,128)(2,1)S(1)}, bf16[256,1536]{1,0:T(8,128)(2,1)}, u32[]{:S(2)}) copy-start(bf16[256,1536]{1,0:T(8,128)(2,1)} %param.23) | copy-start | bytes 2359300
  34.5 228.2 %reduce-scatter.14.cloned.1.call-start = ((), (), s32[]{:S(2)}) async-start(), calls=%async_computation.15 | async-start | bytes 10485760 | tf_op jit(solution)/shard_map/reduce_scatter | solution.py:157
  51.6 628.5 %reduce-scatter.8.cloned.1.call-start = ((), (), s32[]{:S(2)}) async-start(), calls=%async_computation.8 | async-start | bytes 31457280 | tf_op jit(solution)/shard_map/reduce_scatter | solution.py:82
  93.1 1143.1 %reduce-scatter.10.cloned.1.call-start = ((), (), s32[]{:S(2)}) async-start(), calls=%async_computation.11 | async-start | bytes 41943040 | tf_op jit(solution)/shard_map/reduce_scatter | solution.py:88
  131.3 1660.1 %reduce-scatter.18.cloned.1.call-start = ((), (), s32[]{:S(2)}) async-start(), calls=%async_computation.18 | async-start | bytes 41943040 | tf_op jit(solution)/shard_map/reduce_scatter | solution.py:158
  146.3 533.8 %copy-start.29 = (f32[1536]{0:T(1024)S(1)}, f32[1536]{0:T(1024)}, u32[]{:S(2)}) copy-start(f32[1536]{0:T(1024)} %param.24) | copy-start | bytes 18436
  146.3 1865.7 %all-gather.18.cloned.1.call-start = ((), (), s32[]{:S(2)}) async-start(), calls=%async_computation.16 | async-start | bytes 15728640 | tf_op jit(solution)/shard_map/all_gather | solution.py:214
  147.4 548.4 %copy-start.19 = (f32[1024,8]{0,1:T(8,128)}, f32[1024,8]{0,1:T(8,128)S(1)}, u32[]{:S(2)}) copy-start(f32[1024,8]{0,1:T(8,128)S(1)} %get-tuple-element.338) | copy-start | bytes 98308
  885.7 905.7 %copy-start.28 = (f32[2048]{0:T(1024)S(1)}, f32[2048]{0:T(1024)}, u32[]{:S(2)}) copy-start(f32[2048]{0:T(1024)} %param.28) | copy-start | bytes 24580
  889.4 1409.2 %all-gather.14.cloned.1.call-start = ((), (), s32[]{:S(2)}) async-start(), calls=%async_computation.12 | async-start | bytes 20971520 | tf_op jit(solution)/shard_map/all_gather | solution.py:145
  1824.7 187.3 %copy-start.18 = (bf16[256,1536]{1,0:T(8,128)(2,1)S(1)}, bf16[256,1536]{1,0:T(8,128)(2,1)}, u32[]{:S(2)}) copy-start(bf16[256,1536]{1,0:T(8,128)(2,1)} %param.23) | copy-start | bytes 2359300
  1824.8 555.0 %all-gather.10.cloned.1.call-start = ((), (), s32[]{:S(2)}) async-start(), calls=%async_computation.9 | async-start | bytes 5242880 | tf_op jit(solution)/shard_map/all_gather | solution.py:144
  1827.2 839.6 %all-gather.20.cloned.1.call-start = ((), (), s32[]{:S(2)}) async-start(), calls=%async_computation.19 | async-start | bytes 20971520 | tf_op jit(solution)/shard_map/all_gather | solution.py:215
  1827.9 909.0 %reduce-scatter.16.cloned.1.call-start = ((), (), s32[]{:S(2)}) async-start(), calls=%async_computation.17 | async-start | bytes 6291456 | tf_op jit(solution)/shard_map/reduce_scatter | solution.py:222
  2022.5 357.2 %copy-start.13 = (bf16[512,256]{1,0:T(8,128)(2,1)S(1)}, bf16[512,256]{1,0:T(8,128)(2,1)}, u32[]{:S(2)}) copy-start(bf16[512,256]{1,0:T(8,128)(2,1)} %param.25) | copy-start | bytes 786436
  2022.6 755.6 %reduce-scatter.12.cloned.1.call-start = ((), (), s32[]{:S(2)}) async-start(), calls=%async_computation.13 | async-start | bytes 6291456 | tf_op jit(solution)/shard_map/reduce_scatter | solution.py:150
  2386.5 292.9 %copy-start.6 = (bf16[4096,256]{1,0:T(8,128)(2,1)S(1)}, bf16[4096,256]{1,0:T(8,128)(2,1)}, u32[]{:S(2)}) copy-start(bf16[4096,256]{1,0:T(8,128)(2,1)} %all-gather.16.cloned.1.call-done) | copy-start | bytes 6291460
  2386.5 448.2 %reduce-scatter.20.cloned.1.call-start = ((), (), s32[]{:S(2)}) async-start(), calls=%async_computation.20 | async-start | bytes 6291456 | tf_op jit(solution)/shard_map/reduce_scatter | solution.py:223
  2679.3 279.3 %all-reduce.7.cloned.1.call-start = ((), (), s32[]{:S(2)}) async-start(), calls=%async_computation.21 | async-start | bytes 12582912 | tf_op jit(solution)/shard_map/psum | solution.py:242
  2716.9 117.8 %copy-start.7 = (bf16[2048,256]{1,0:T(8,128)(2,1)S(1)}, bf16[2048,256]{1,0:T(8,128)(2,1)}, u32[]{:S(2)}) copy-start(bf16[2048,256]{1,0:T(8,128)(2,1)} %param.18) | copy-start | bytes 3145732
  2716.9 117.8 %copy-start.25 = (f32[2048]{0:T(1024)S(1)}, f32[2048]{0:T(1024)}, u32[]{:S(2)}) copy-start(f32[2048]{0:T(1024)} %copy-done.24) | copy-start | bytes 24580
  2716.9 117.8 %copy-start.27 = (f32[2048]{0:T(1024)S(1)}, f32[2048]{0:T(1024)}, u32[]{:S(2)}) copy-start(f32[2048]{0:T(1024)} %copy-done.26) | copy-start | bytes 24580
  2716.9 117.8 %copy-start.30 = (f32[256]{0:T(256)S(1)}, f32[256]{0:T(256)}, u32[]{:S(2)}) copy-start(f32[256]{0:T(256)} %param.19) | copy-start | bytes 3076
  2716.9 117.8 %copy-start.31 = (f32[256]{0:T(256)S(1)}, f32[256]{0:T(256)}, u32[]{:S(2)}) copy-start(f32[256]{0:T(256)} %param.21) | copy-start | bytes 3076
  2716.9 117.8 %copy-start.32 = (f32[256]{0:T(256)S(1)}, f32[256]{0:T(256)}, u32[]{:S(2)}) copy-start(f32[256]{0:T(256)} %param.30) | copy-start | bytes 3076
  2717.0 117.8 %copy-start.33 = (f32[256]{0:T(256)S(1)}, f32[256]{0:T(256)}, u32[]{:S(2)}) copy-start(f32[256]{0:T(256)} %param.26) | copy-start | bytes 3076
  2724.5 147.3 %copy-start.9 = (bf16[2048,256]{1,0:T(8,128)(2,1)S(1)}, bf16[2048,256]{1,0:T(8,128)(2,1)}, u32[]{:S(2)}) copy-start(bf16[2048,256]{1,0:T(8,128)(2,1)} %param.31) | copy-start | bytes 3145732
  2736.9 225.0 %copy-start.34 = (f32[256]{0:T(256)}, f32[256]{0:T(256)S(1)}, u32[]{:S(2)}) copy-start(f32[256]{0:T(256)S(1)} %get-tuple-element.571) | copy-start | bytes 3076
  (30 other events, 274.9 us)
Sparse Core Ops, SparseCore 0:
  9.6 35.8 all-gather.15
  47.5 33.1 all-gather.7
  82.8 33.1 all-gather.11
  118.2 144.4 reduce-scatter.13
  264.9 415.1 reduce-scatter.7
  682.4 553.8 reduce-scatter.9
  1238.6 552.7 reduce-scatter.17
  1793.1 218.9 all-gather.17
  2013.7 284.9 all-gather.13
  2300.8 78.9 all-gather.9
  2381.4 285.2 all-gather.19
  2669.0 52.4 reduce-scatter.15
  2723.8 54.2 reduce-scatter.11
  2780.4 54.2 reduce-scatter.19
  2838.3 120.2 all-reduce.6
where the time goes:
time: 2990 us; the launch traced here: 2980 us
  waiting for transfers between devices  2490 us (83%)
  matrix products  198 us (7%)
  other arithmetic  113 us (4%)
  local copies, waits for them, and re-layouts  86.7 us (3%)
  blocking collectives  65 us (2%)
    reduce_scatter x1, waiting for transfers between devices, local(): lax.psum_scatter(trailing(grad_rows, w_down), 'gy', scatter_dimension=0,...  555 us
    reduce_scatter x1, waiting for transfers between devices, local(): lax.psum_scatter(jnp.dot(attn_rows, w_qkv, preferred_element_type=jnp.flo...  414 us
    reduce_scatter x1, waiting for transfers between devices, local(): lax.psum_scatter(jnp.dot(mlp_rows, w_up, preferred_element_type=jnp.float...  347 us
    all_gather x1, waiting for transfers between devices, local(): lax.all_gather(grad_pre, 'gy', axis=0, tiled=True)  280 us
    all_gather x1, waiting for transfers between devices, local(): lax.all_gather(act_low, 'gy', axis=0, tiled=True)  276 us
    all_gather x1, waiting for transfers between devices, local(): lax.all_gather(grad_qkv, 'gy', axis=0, tiled=True)  184 us
    reduce_scatter x1, waiting for transfers between devices, local(): lax.psum_scatter(trailing(grad_rows, w_dense), 'gy', scatter_dimension=0,...  115 us
    psum x1, waiting for transfers between devices, local(): lax.psum((grad_w_qkv, grad_b_qkv, grad_w_dense, grad_b_out, grad_w_up, gr...  82.7 us
  transfers between devices with their start and end apart: 15, of which 14 were waited for; matrix products, arithmetic and copies ran while one was open for 13% of the time, Pallas kernels for 0%

commit v1 on v0

v1 whole, which is shorter than its diff:
```python
import functools

import jax
import jax.numpy as jnp
from jax import lax
from jax.experimental import pallas as pl
from jax.experimental.pallas import tpu as pltpu
from jax.sharding import PartitionSpec as P

HD = 64
ROT = 16
LEN = 1024
EPS = 1e-05
F32 = jnp.float32
BF16 = jnp.bfloat16


def mm(left, right):
    return jnp.dot(left, right, preferred_element_type=F32)


def mm_t(left, right):
    return lax.dot_general(left, right, (((1,), (1,)), ((), ())), preferred_element_type=F32)


def t_mm(left, right):
    return lax.dot_general(left, right, (((0,), (0,)), ((), ())), preferred_element_type=F32)


def swap(value, axis, step, count):
    return lax.ppermute(value, axis, [(i, i ^ step) for i in range(count)])


def xor_order(value, index, count):
    rest = value.shape[1:]
    bit = 1
    while bit < count:
        paired = value.reshape((count // (2 * bit), 2, bit) + rest)
        turned = paired[:, ::-1]
        value = jnp.where((index & bit) != 0, turned, paired).reshape((count,) + rest)
        bit *= 2
    return value


def rope_tables(width):
    places = jnp.arange(LEN).astype(F32)
    freqs = 10000.0 ** (-jnp.arange(ROT // 2).astype(F32) * 2.0 / ROT)
    turned = places[:, None] * freqs[None, :]
    cosine, sine = jnp.cos(turned), jnp.sin(turned)
    rest = HD - ROT
    zeros = jnp.zeros_like(sine)
    keep = jnp.concatenate([cosine, cosine, jnp.ones((LEN, rest), F32)], axis=1)
    from_up = jnp.concatenate([-sine, zeros, jnp.zeros((LEN, rest), F32)], axis=1)
    from_down = jnp.concatenate([zeros, sine, jnp.zeros((LEN, rest), F32)], axis=1)
    return tuple(jnp.tile(part, (1, width // HD)) for part in (keep, from_up, from_down))


def attention_kernel(
    width, x_ref, wq_ref, b_ref, g_ref, wd_ref, keep_ref, up_ref, down_ref,
    heads_ref, dqkv_ref, db_ref, q_s, k_s, v_s, g_s, kt_s, vt_s, dk_s, dv_s,
):
    heads = width // HD
    half = ROT // 2
    block = 256
    scale = HD ** (-0.5)
    b_row = b_ref[...]

    def turn(value, rows, sign):
        return (
            value * keep_ref[rows, :]
            + sign * (pltpu.roll(value, width - half, 1) * up_ref[rows, :])
            + sign * (pltpu.roll(value, half, 1) * down_ref[rows, :])
        )

    for part in range(LEN // block):
        rows = pl.ds(part * block, block)
        proj = mm(x_ref[rows, :], wq_ref[...]) + b_row
        q_s[rows, :] = turn(proj[:, :width], rows, 1.0).astype(BF16)
        key = turn(proj[:, width : 2 * width], rows, 1.0)
        value = proj[:, 2 * width :]
        k_s[rows, :] = key.astype(BF16)
        v_s[rows, :] = value.astype(BF16)
        kt_s[:, rows] = key.T.astype(BF16)
        vt_s[:, rows] = value.T.astype(BF16)
        g_s[rows, :] = mm(g_ref[rows, :], wd_ref[...]).astype(BF16)

    dk_s[...] = jnp.zeros_like(dk_s)
    dv_s[...] = jnp.zeros_like(dv_s)
    lane_head = lax.broadcasted_iota(jnp.int32, (block, width), 1) // HD
    key_at = lax.broadcasted_iota(jnp.int32, (block, block), 0)
    query_at = lax.broadcasted_iota(jnp.int32, (block, block), 1)
    seen = key_at <= query_at
    db_q = jnp.zeros((1, width), F32)
    for part in range(LEN // block):
        rows = pl.ds(part * block, block)
        span = (part + 1) * block
        q_block, g_block = q_s[rows, :], g_s[rows, :]
        outs, dqs = [], []
        dk_new, dv_new = None, None
        for head in range(heads):
            own = lane_head == head
            q_own = jnp.where(own, q_block, jnp.zeros_like(q_block))
            g_own = jnp.where(own, g_block, jnp.zeros_like(g_block))
            scores = mm_t(k_s[:span, :], q_own)
            last = jnp.where(seen, scores[span - block :, :], -1e30)
            scores = last if part == 0 else jnp.concatenate([scores[: span - block, :], last], axis=0)
            top = jnp.max(scores, axis=0, keepdims=True)
            exponent = jnp.exp((scores - top) * scale)
            weights = exponent * (1.0 / jnp.sum(exponent, axis=0, keepdims=True))
            low = weights.astype(BF16)
            dweights = mm_t(v_s[:span, :], g_own)
            inner = jnp.sum(weights * dweights, axis=0, keepdims=True)
            dscores = (weights * (dweights - inner)).astype(BF16)
            at = slice(head * HD, (head + 1) * HD)
            outs.append(mm(vt_s[at, :span], low))
            dqs.append(mm(kt_s[at, :span], dscores))
            dv_here, dk_here = mm(low, g_own), mm(dscores, q_own)
            dv_new = dv_here if dv_new is None else dv_new + dv_here
            dk_new = dk_here if dk_new is None else dk_new + dk_here
        dk_s[:span, :] += dk_new
        dv_s[:span, :] += dv_new
        heads_ref[rows, :] = jnp.concatenate(outs, axis=0).T.astype(BF16)
        dq = jnp.concatenate(dqs, axis=0).T * scale
        dq_low = turn(dq, rows, -1.0).astype(BF16)
        dqkv_ref[rows, :width] = dq_low
        db_q = db_q + jnp.sum(dq_low.astype(F32), axis=0, keepdims=True)
    db_k = jnp.zeros((1, width), F32)
    db_v = jnp.zeros((1, width), F32)
    for part in range(LEN // block):
        rows = pl.ds(part * block, block)
        dk_low = turn(dk_s[rows, :] * scale, rows, -1.0).astype(BF16)
        dv_low = dv_s[rows, :].astype(BF16)
        dqkv_ref[rows, width : 2 * width] = dk_low
        dqkv_ref[rows, 2 * width :] = dv_low
        db_k = db_k + jnp.sum(dk_low.astype(F32), axis=0, keepdims=True)
        db_v = db_v + jnp.sum(dv_low.astype(F32), axis=0, keepdims=True)
    db_ref[:, :width] = db_q
    db_ref[:, width : 2 * width] = db_k
    db_ref[:, 2 * width :] = db_v


def attention_fused(attn_in, w_qkv, b_qkv, grad, w_dense_t, tables):
    width = w_dense_t.shape[1]
    features = attn_in.shape[1]
    return pl.pallas_call(
        functools.partial(attention_kernel, width),
        out_shape=(
            jax.ShapeDtypeStruct((LEN, width), BF16),
            jax.ShapeDtypeStruct((LEN, 3 * width), BF16),
            jax.ShapeDtypeStruct((1, 3 * width), F32),
        ),
        in_specs=[pl.BlockSpec(memory_space=pltpu.VMEM)] * 8,
        out_specs=tuple([pl.BlockSpec(memory_space=pltpu.VMEM)] * 3),
        scratch_shapes=[
            pltpu.VMEM((LEN, width), BF16),
            pltpu.VMEM((LEN, width), BF16),
            pltpu.VMEM((LEN, width), BF16),
            pltpu.VMEM((LEN, width), BF16),
            pltpu.VMEM((width, LEN), BF16),
            pltpu.VMEM((width, LEN), BF16),
            pltpu.VMEM((LEN, width), F32),
            pltpu.VMEM((LEN, width), F32),
        ],
        compiler_params=pltpu.CompilerParams(vmem_limit_bytes=48 * 1024 * 1024),
        cost_estimate=pl.CostEstimate(
            flops=2 * LEN * features * 4 * width + 20 * LEN * LEN * width,
            bytes_accessed=4 * LEN * features + 20 * LEN * width,
            transcendentals=LEN * LEN * width // HD,
        ),
    )(attn_in, w_qkv, b_qkv.reshape(1, -1), grad, w_dense_t, *tables)


def attention_plain(attn_in, w_qkv, b_qkv, grad, w_dense_t, tables):
    width = w_dense_t.shape[1]
    heads = width // HD
    keep, up, down = tables
    half = ROT // 2

    def turn(value, sign):
        return value * keep + sign * (
            jnp.roll(value, -half, 1) * up + jnp.roll(value, half, 1) * down
        )

    def split(value):
        return value.reshape(LEN, heads, HD)

    def product(pattern, left, right):
        return jnp.einsum(pattern, left, right, preferred_element_type=F32)

    proj = mm(attn_in, w_qkv) + b_qkv
    query = split(turn(proj[:, :width], 1.0).astype(BF16))
    key = split(turn(proj[:, width : 2 * width], 1.0).astype(BF16))
    value = split(proj[:, 2 * width :].astype(BF16))
    grad_low = split(mm(grad, w_dense_t).astype(BF16))
    places = jnp.arange(LEN)
    scores = product("qhe,khe->hqk", query, key) * HD ** (-0.5)
    weights = jax.nn.softmax(jnp.where(places[:, None] >= places[None, :], scores, -1e30), axis=-1)
    low = weights.astype(BF16)
    mixed = product("hqk,khe->qhe", low, value).reshape(LEN, width).astype(BF16)
    dweights = product("qhe,khe->hqk", grad_low, value)
    inner = jnp.sum(weights * dweights, axis=-1, keepdims=True)
    dscores = (weights * (dweights - inner)).astype(BF16)
    dq = product("hqk,khe->qhe", dscores, key).reshape(LEN, width) * HD ** (-0.5)
    dk = product("hqk,qhe->khe", dscores, query).reshape(LEN, width) * HD ** (-0.5)
    dv = product("hqk,qhe->khe", low, grad_low).reshape(LEN, width)
    dqkv = jnp.concatenate([turn(dq, -1.0), turn(dk, -1.0), dv], axis=1).astype(BF16)
    return mixed, dqkv, jnp.sum(dqkv.astype(F32), axis=0, keepdims=True)


def normalize(hidden):
    inputs = hidden.astype(F32)
    mean = jnp.mean(inputs, axis=1, keepdims=True)
    square = jnp.mean(inputs * inputs, axis=1, keepdims=True)
    inv_std = lax.rsqrt(square - mean * mean + EPS)
    return (inputs - mean) * inv_std, inv_std


def feed_forward(mlp_in, w_up, b_up, grad, w_down_t):
    pre = mm(mlp_in, w_up) + b_up
    grad_act = mm(grad, w_down_t)
    phi = 0.5 * (1.0 + lax.erf(pre * (0.5 ** 0.5)))
    slope = phi + pre * (jnp.exp(-0.5 * pre * pre) * 0.3989422804014327)
    act = (pre * phi).astype(BF16)
    dpre = (slope * grad_act).astype(BF16)
    return act, dpre, jnp.sum(dpre.astype(F32), axis=0, keepdims=True)


def sequence_pass(hidden, grad, gains, chunks, reduce_chunk):
    normed, inv_std = normalize(hidden)
    attn_in = (normed * gains[0] + gains[1]).astype(BF16)
    mlp_in = (normed * gains[2] + gains[3]).astype(BF16)
    width = chunks[0][2].shape[1]
    fused = width % 128 == 0
    tables = rope_tables(width)
    branch = grad_attn = grad_mlp = None
    weight_grads, bias_grads = [], []

    def add(total, term):
        return term if total is None else total + term

    ffn, att = [], []
    for w_qkv, b_qkv, w_dense_t, w_up, b_up, w_down_t in chunks:
        act, dpre, db_up = feed_forward(mlp_in, w_up, b_up, grad, w_down_t)
        branch = add(branch, mm_t(act, w_down_t))
        grad_mlp = add(grad_mlp, mm_t(dpre, w_up))
        ffn.append((t_mm(mlp_in, dpre), t_mm(grad, act), db_up))
    for w_qkv, b_qkv, w_dense_t, w_up, b_up, w_down_t in chunks:
        attention = attention_fused if fused else attention_plain
        mixed, dqkv, db_qkv = attention(attn_in, w_qkv, b_qkv, grad, w_dense_t, tables)
        branch = add(branch, mm_t(mixed, w_dense_t))
        grad_attn = add(grad_attn, mm_t(dqkv, w_qkv))
        att.append((t_mm(attn_in, dqkv), t_mm(grad, mixed), db_qkv))
    ups = reduce_chunk([item[0] for item in ffn])
    downs = reduce_chunk([item[1] for item in ffn])
    qkvs = reduce_chunk([item[0] for item in att])
    denses = reduce_chunk([item[1] for item in att])
    db_up = jnp.concatenate([item[2] for item in ffn], axis=0)
    db_qkv = jnp.concatenate([item[2] for item in att], axis=0)
    sums = jnp.stack(
        [
            jnp.sum(grad_attn * normed, axis=0),
            jnp.sum(grad_attn, axis=0),
            jnp.sum(grad_mlp * normed, axis=0),
            jnp.sum(grad_mlp, axis=0),
            jnp.sum(grad.astype(F32), axis=0),
        ]
    )
    grad_normed = grad_attn * gains[0] + grad_mlp * gains[2]
    row_sums = jnp.stack([jnp.sum(grad_normed, axis=1), jnp.sum(grad_normed * normed, axis=1)], axis=0)
    return normed, inv_std, branch, grad_normed, row_sums, sums, (qkvs, denses, ups, downs), db_qkv, db_up


def by_part(weight, heads):
    rows = weight.shape[0]
    return weight.reshape(rows, heads, 3, HD).transpose(0, 2, 1, 3).reshape(rows, -1)


def by_head(weight, heads):
    rows = weight.shape[0]
    return weight.reshape(rows, 3, heads, HD).transpose(0, 2, 1, 3).reshape(rows, -1)


def local_box(
    hidden_in, ln1_gain, ln1_bias, ln2_gain, ln2_bias, w_qkv, b_qkv, w_dense, b_dense, w_up, b_up,
    w_down, b_down, cotangent,
):
    dp, gx, gy = lax.axis_index("dp"), lax.axis_index("gx"), lax.axis_index("gy")
    wide = hidden_in.shape[1]
    half = wide // 2
    lower = gx == 0
    aligned = (gy // 2) == gx
    odd = (gy % 2) == 1

    def rel_rows(value):
        return jnp.where(lower, value, jnp.roll(value, -half, axis=0))

    def gather_z(value):
        return jnp.concatenate([value] + [swap(value, "gy", k, 4) for k in (1, 2, 3)], axis=0)

    def to_half(value):
        value = value.reshape(2, LEN, wide)
        first, second = value[:, :, :half], value[:, :, half:]
        kept = jnp.where(lower, first, second)
        got = swap(jnp.where(lower, second, first), "gx", 1, 2)
        near = jnp.where(aligned, kept, got)
        far = jnp.where(aligned, got, kept)
        near = jnp.where(odd, near[::-1], near)
        far = jnp.where(odd, far[::-1], far)
        pieces = [near[0], near[1], far[0], far[1]]
        return [pieces[0]] + [swap(pieces[k], "gy", k, 4) for k in (1, 2, 3)]

    def whole_rows(mine):
        other = [swap(piece, "gx", 1, 2) for piece in mine]
        return jnp.concatenate([part for pair in zip(mine, other) for part in pair], axis=1)

    def from_half(pieces):
        got = [pieces[0]] + [swap(pieces[k], "gy", k, 4) for k in (1, 2, 3)]
        near, far = jnp.stack(got[:2]), jnp.stack(got[2:])
        own = jnp.where(aligned, near, far)
        gone = jnp.where(aligned, far, near)
        own = jnp.where(odd, own[::-1], own)
        gone = jnp.where(odd, gone[::-1], gone)
        back = swap(gone, "gx", 1, 2)
        first = jnp.where(lower, own, back)
        second = jnp.where(lower, back, own)
        return jnp.concatenate([first, second], axis=2).reshape(2 * LEN, wide)

    hidden_half = to_half(hidden_in)
    hidden = whole_rows(hidden_half)
    grad_half = to_half(cotangent)
    grad = whole_rows(grad_half)

    vectors = jnp.stack([ln1_gain, ln1_bias, ln2_gain, ln2_bias, b_dense + b_down])
    vectors = rel_rows(vectors.T).T
    vectors = jnp.concatenate([vectors] + [swap(vectors, "gy", k, 4) for k in (1, 2, 3)], axis=1)

    heads = w_qkv.shape[1] // (3 * HD) // 4

    def quarter(value):
        columns = value.shape[1] // 4
        return lax.dynamic_slice_in_dim(value, dp * columns, columns, 1)

    def spread(value):
        block = gather_z(rel_rows(value))
        core = swap(block, "dp", 1, 4)
        across = swap(block, "dp", 2, 4)
        return [block, core, across, swap(across, "dp", 1, 4)]

    w_qkv_c = spread(by_part(quarter(w_qkv), heads))
    w_up_c = spread(quarter(w_up))
    w_dense_c = spread(lax.dynamic_slice_in_dim(w_dense, dp * (w_dense.shape[0] // 4), w_dense.shape[0] // 4, 0).T)
    w_down_c = spread(lax.dynamic_slice_in_dim(w_down, dp * (w_down.shape[0] // 4), w_down.shape[0] // 4, 0).T)
    b_qkv_c = xor_order(by_part(b_qkv.reshape(4, -1), heads), dp, 4)
    b_up_c = xor_order(b_up.reshape(4, -1), dp, 4)
    chunks = [
        (w_qkv_c[k], b_qkv_c[k], w_dense_c[k], w_up_c[k], b_up_c[k], w_down_c[k]) for k in range(4)
    ]

    def reduce_chunk(grads):
        sum_far = grads[2] + swap(grads[3].astype(BF16), "dp", 1, 4).astype(F32)
        sum_near = grads[0] + swap(grads[1].astype(BF16), "dp", 1, 4).astype(F32)
        total = sum_near + swap(sum_far.astype(BF16), "dp", 2, 4).astype(F32)
        blocks = total.reshape(4, wide, -1)
        low = blocks.astype(BF16)
        mine = blocks[0]
        for k in (1, 2, 3):
            mine = mine + swap(low[k], "gy", k, 4).astype(F32)
        mine = rel_rows(mine.astype(BF16))
        across = swap(mine, "dp", 2, 4)
        quarters = jnp.stack([mine, swap(mine, "dp", 1, 4), across, swap(across, "dp", 1, 4)])
        return xor_order(quarters, dp, 4)

    normed, inv_std, branch, grad_normed, row_sums, sums, reduced, db_qkv, db_up = sequence_pass(
        hidden, grad, vectors, chunks, reduce_chunk
    )

    def halves(value, which):
        return [value[:, (2 * k + which) * half : (2 * k + which + 1) * half] for k in range(4)]

    sent = [swap(part.astype(BF16), "gx", 1, 2) for part in halves(branch, 1)]
    bias_half = halves(vectors[4:5], 0)
    out_half = [
        (hidden_half[k].astype(F32) + part + sent[k].astype(F32) + bias_half[k]).astype(BF16)
        for k, part in enumerate(halves(branch, 0))
    ]
    hidden_out = from_half(out_half)

    features = 4 * wide
    row_sums = row_sums + swap(row_sums, "gx", 1, 2)
    mean_total = row_sums[0][:, None] / features
    mean_cross = row_sums[1][:, None] / features
    sent = [swap(part.astype(BF16), "gx", 1, 2) for part in halves(grad_normed, 1)]
    normed_half = halves(normed, 0)
    in_half = [
        (
            grad_half[k].astype(F32)
            + inv_std * (part + sent[k].astype(F32) - mean_total - normed_half[k] * mean_cross)
        ).astype(BF16)
        for k, part in enumerate(halves(grad_normed, 0))
    ]
    grad_input = from_half(in_half)

    sums = sums * jnp.array([1.0, 1.0, 1.0, 1.0, 0.5], F32)[:, None]
    mine = sums[:, :wide]
    for k in (1, 2, 3):
        mine = mine + swap(sums[:, k * wide : (k + 1) * wide], "gy", k, 4)
    mine = rel_rows(mine.T).T
    mine = mine + swap(mine, "gx", 1, 2)
    db = jnp.concatenate([xor_order(by_head(db_qkv, heads), dp, 4).reshape(-1), xor_order(db_up, dp, 4).reshape(-1)])
    db = db + swap(db, "gy", 1, 4)
    db = db + swap(db, "gy", 2, 4)
    both = jnp.concatenate([mine.reshape(-1), db])
    both = both + swap(both, "dp", 1, 4)
    both = both + swap(both, "dp", 2, 4)
    mine = both[: 5 * wide].reshape(5, wide)
    columns = w_qkv.shape[1]
    grad_b_qkv = both[5 * wide : 5 * wide + columns]
    grad_b_up = both[5 * wide + columns :]

    qkvs, denses, ups, downs = reduced

    def joined(quarters):
        return quarters.transpose(1, 0, 2).reshape(wide, -1).astype(F32)

    grad_w_qkv = joined(by_head(qkvs.reshape(4 * wide, -1), heads).reshape(4, wide, -1))
    grad_w_up = joined(ups)
    grad_w_dense = denses.transpose(0, 2, 1).reshape(-1, wide).astype(F32)
    grad_w_down = downs.transpose(0, 2, 1).reshape(-1, wide).astype(F32)
    return (
        hidden_out, grad_input, mine[0], mine[1], mine[2], mine[3], grad_w_qkv, grad_b_qkv,
        grad_w_dense, mine[4], grad_w_up, grad_b_up, grad_w_down, mine[4],
    )


def local_any(
    gx_count, gy_count,
    hidden_in, ln1_gain, ln1_bias, ln2_gain, ln2_bias, w_qkv, b_qkv, w_dense, b_dense, w_up, b_up,
    w_down, b_down, cotangent,
):
    heads = w_qkv.shape[1] // (3 * HD)

    def to_sequence(value):
        rows = lax.all_gather(value, "gx", axis=0, tiled=True)
        return lax.all_to_all(rows, "gy", split_axis=0, concat_axis=1, tiled=True)

    def from_sequence(value):
        return lax.all_to_all(value, "gy", split_axis=1, concat_axis=0, tiled=True)

    def gather(value):
        return lax.all_gather(value, "gy", axis=0, tiled=True)

    hidden, grad = to_sequence(hidden_in), to_sequence(cotangent)
    vectors = jnp.stack([ln1_gain, ln1_bias, ln2_gain, ln2_bias])
    vectors = lax.all_gather(vectors, "gy", axis=1, tiled=True)
    chunk = (
        gather(by_part(w_qkv, heads)),
        by_part(b_qkv[None], heads)[0],
        gather(w_dense.T),
        gather(w_up),
        b_up,
        gather(w_down.T),
    )

    def reduce_chunk(grads):
        return lax.psum(lax.psum_scatter(grads[0], "gy", scatter_dimension=0, tiled=True), "dp")

    normed, inv_std, branch, grad_normed, row_sums, sums, reduced, db_qkv, db_up = sequence_pass(
        hidden, grad, vectors, [chunk], reduce_chunk
    )
    branch_rows = lax.psum_scatter(from_sequence(branch), "gx", scatter_dimension=0, tiled=True)
    hidden_out = (hidden_in.astype(F32) + branch_rows + b_dense + b_down).astype(BF16)
    features = normed.shape[1]
    row_sums = lax.psum(row_sums, "gx")
    grad_normed = grad_normed - (
        row_sums[0][:, None] / features + normed * (row_sums[1][:, None] / features)
    ) * (1.0 / gx_count)
    grad_rows = lax.psum_scatter(from_sequence(inv_std * grad_normed), "gx", scatter_dimension=0, tiled=True)
    grad_input = (cotangent.astype(F32) + grad_rows).astype(BF16)
    sums = lax.psum_scatter(sums, "gy", scatter_dimension=1, tiled=True)
    sums = lax.psum(sums * jnp.array([1.0] * 4 + [1.0 / gx_count], F32)[:, None], ("dp", "gx"))
    db_qkv, db_up = lax.psum((by_head(db_qkv, heads)[0], db_up[0]), ("dp", "gy"))
    qkvs, denses, ups, downs = reduced
    return (
        hidden_out, grad_input, sums[0], sums[1], sums[2], sums[3], by_head(qkvs, heads), db_qkv,
        denses.T, sums[4], ups, db_up, downs.T, sums[4],
    )


def solution(mesh):
    sizes = mesh.shape
    boxed = sizes["dp"] == 4 and sizes["gx"] == 2 and sizes["gy"] == 4
    rows, feature = P(("dp", "gx"), "gy"), P("gy")
    placed = (
        rows, feature, feature, feature, feature, P("gy", "gx"), P("gx"), P("gx", "gy"), feature,
        P("gy", "gx"), P("gx"), P("gx", "gy"), feature, rows,
    )
    return jax.shard_map(
        local_box if boxed else functools.partial(local_any, sizes["gx"], sizes["gy"]),
        mesh=mesh,
        in_specs=placed,
        out_specs=(rows, rows) + placed[1:5] + placed[5:13],
        check_vma=False,
    )
```

time: 2990 us -> 611 us (0.20)
  waiting for transfers between devices: 2490 us -> 197 us
  starting transfers between devices: 1.17 us -> 122 us
  other arithmetic: 113 us -> 38.3 us
  matrix products: 198 us -> 132 us
  blocking collectives: 65 us -> 0 us
  Pallas kernels: 0 us -> 42.1 us
    reduce_scatter x7 -> x0, waiting for transfers between devices: 1530 us -> none  [the longest x1 555 us: local(): lax.psum_scatter(trailing(grad_rows, w_down), 'gy', scatter_dimension=0,...]
    all_gather x7 -> x0, waiting for transfers between devices: 874 us -> none  [the longest x1 280 us: local(): lax.all_gather(grad_pre, 'gy', axis=0, tiled=True)]
    ppermute x0 -> x104, waiting for transfers between devices: none -> 197 us  [swap(): return lax.ppermute(value, axis, [(i, i ^ step) for i in range(count)])]
    ppermute x0 -> x104, starting transfers between devices: none -> 122 us  [swap(): return lax.ppermute(value, axis, [(i, i ^ step) for i in range(count)])]
    psum x1 -> x0, waiting for transfers between devices: 82.7 us -> none  [local(): lax.psum((grad_w_qkv, grad_b_qkv, grad_w_dense, grad_b_out, grad_w_up, gr...]
    dot_general x26 -> x40, matrix products: 198 us -> 132 us  [the longest x16 67 us: mm_t(): lax.dot_general(left, right, (((1,), (1,)), ((), ())), preferred_element_...]
    psum x4 -> x0, blocking collectives: 65 us -> none  [the longest x1 20.5 us: local(): lax.psum((jnp.sum(inputs, axis=1), jnp.sum(inputs * inputs, axis=1)), 'gy')]
    convert_element_type x8 -> x10, other arithmetic: 61.6 us -> 6.11 us  [the longest x1 1.57 us: local_box(): grad_w_down = downs.transpose(0, 2, 1).reshape(-1, wide).astype(F32)]
  transfers between devices with their start and end apart: 15 -> 104, of which waited for: 14 -> 39; matrix products, arithmetic and copies ran while one was open for 13% -> 37% of each run, Pallas kernels for 0% -> 7%
where the time goes in v1:
time: 611 us; the launch traced here: 601 us
  waiting for transfers between devices  197 us (32%)
  matrix products  132 us (22%)
  starting transfers between devices  122 us (20%)
  local copies, waits for them, and re-layouts  67 us (11%)
  Pallas kernels  42.1 us (7%)
  other arithmetic  38.3 us (6%)
    ppermute x104, waiting for transfers between devices, swap(): return lax.ppermute(value, axis, [(i, i ^ step) for i in range(count)])  197 us
    ppermute x104, starting transfers between devices, swap(): return lax.ppermute(value, axis, [(i, i ^ step) for i in range(count)])  122 us
    dot_general x16, matrix products, mm_t(): lax.dot_general(left, right, (((1,), (1,)), ((), ())), preferred_element_...  67 us
    pallas_call x4, Pallas kernels, attention_fused(): pl.pallas_call(functools.partial(attention_kernel, width), out_shape=(jax...  42.1 us
    dot_general x16, matrix products, t_mm(): lax.dot_general(left, right, (((0,), (0,)), ((), ())), preferred_element_...  39.9 us
    dot_general x8, matrix products, mm(): return jnp.dot(left, right, preferred_element_type=F32)  24.8 us
    unnamed x214, local copies, waits for them, and re-layouts  17 us
  transfers between devices with their start and end apart: 104, of which 39 were waited for; matrix products, arithmetic and copies ran while one was open for 37% of the time, Pallas kernels for 7%

profile of v1, /device:TPU:0, one launch (start us, length us, event | category | flops | bytes accessed | tf_op | source)
XLA Modules:
  0.0 600.9 jit_solution(3885340055379880763)
XLA Ops:
  2.9 5.0 collective-permute-start.10
  57.6 11.1 %collective-permute-start.23 = (bf16[256,384]{1,0:T(8,128)(2,1)S(1)}, bf16[256,384]{1,0:T(8,128)(2,1)S(1)}, u32[]{:S(2)}, u32[]{:S(2)}) collective-permute-start(bf16[256,384]{1,0:T(8,128)(2,1)S(1)} %maximum_select_fusion.4), channel_id=1, source_target_pairs={{0,1},{1,0},{2,3},{3,2},{4,5},{5,4},{6,7},{7,6},{8,9},{9,8},{10,11... | collective-permute-start | bytes 589832 | tf_op jit(solution)/shard_map/ppermute | solution.py:31
  78.3 11.7 %collective-permute-done.12 = bf16[256,512]{0,1:T(8,128)(2,1)S(1)} collective-permute-done((bf16[256,512]{0,1:T(8,128)(2,1)}, bf16[256,512]{0,1:T(8,128)(2,1)S(1)}, u32[]{:S(2)}, u32[]{:S(2)}) %collective-permute-start.12) | collective-permute-done | bytes 262176 | tf_op jit(solution)/shard_map/ppermute | solution.py:31
  92.8 7.2 %collective-permute-done.15 = bf16[256,512]{0,1:T(8,128)(2,1)S(1)} collective-permute-done((bf16[256,512]{0,1:T(8,128)(2,1)}, bf16[256,512]{0,1:T(8,128)(2,1)S(1)}, u32[]{:S(2)}, u32[]{:S(2)}) %collective-permute-start.15) | collective-permute-done | bytes 262176 | tf_op jit(solution)/shard_map/ppermute | solution.py:31
  111.4 4.8 collective-permute-done.2
  120.5 4.9 collective-permute-done.4
  129.5 5.2 collective-permute-done.5
  142.1 4.7 collective-permute-done.30
  159.3 4.4 collective-permute-done.33
  173.6 10.3 %shard_map.254 = (bf16[1024,128]{1,0:T(8,128)(2,1)S(1)}, bf16[1024,384]{1,0:T(8,128)(2,1)S(1)}, f32[1,384]{1,0:T(1,128)S(1)}) custom-call(bf16[1024,1024]{1,0:T(8,128)(2,1)S(1)} %get-tuple-element.84.x_ref, bf16[1024,384]{1,0:T(8,128)(2,1)S(1)} %pad_maximum_fusion.6.wq_ref, f32[1,384]{1,0:T(1,128)S(1)} %get-tuple-element.171.b_ref, ...), custom_call_target="tpu_custom_call" | custom-call | flops 3758096384 | bytes 6815744 | tf_op jit(solution)/shard_map/pallas_call | solution.py:145
  185.1 10.8 %shard_map.255 = (bf16[1024,128]{1,0:T(8,128)(2,1)S(1)}, bf16[1024,384]{1,0:T(8,128)(2,1)S(1)}, f32[1,384]{1,0:T(1,128)S(1)}) custom-call(bf16[1024,1024]{1,0:T(8,128)(2,1)S(1)} %get-tuple-element.84.x_ref, bf16[1024,384]{1,0:T(8,128)(2,1)S(1)} %collective-permute-done.37.wq_ref, f32[1,384]{1,0:T(1,128)S(1)} %get-tuple-element.170.b_ref, ...), custom_call_target="tpu_custom_call" | custom-call | flops 3758096384 | bytes 6815744 | tf_op jit(solution)/shard_map/pallas_call | solution.py:145
  202.2 10.5 %shard_map.256 = (bf16[1024,128]{1,0:T(8,128)(2,1)S(1)}, bf16[1024,384]{1,0:T(8,128)(2,1)S(1)}, f32[1,384]{1,0:T(1,128)S(1)}) custom-call(bf16[1024,1024]{1,0:T(8,128)(2,1)S(1)} %get-tuple-element.84.x_ref, bf16[1024,384]{1,0:T(8,128)(2,1)S(1)} %collective-permute-done.39.wq_ref, f32[1,384]{1,0:T(1,128)S(1)} %get-tuple-element.169.b_ref, ...), custom_call_target="tpu_custom_call" | custom-call | flops 3758096384 | bytes 6815744 | tf_op jit(solution)/shard_map/pallas_call | solution.py:145
  243.8 4.4 fusion.133
  252.4 5.3 fusion.126
  257.7 4.5 fusion.134
  262.2 4.5 fusion.124
  269.1 10.5 %shard_map.257 = (bf16[1024,128]{1,0:T(8,128)(2,1)S(1)}, bf16[1024,384]{1,0:T(8,128)(2,1)S(1)}, f32[1,384]{1,0:T(1,128)S(1)}) custom-call(bf16[1024,1024]{1,0:T(8,128)(2,1)S(1)} %get-tuple-element.84.x_ref, bf16[1024,384]{1,0:T(8,128)(2,1)S(1)} %collective-permute-done.41.wq_ref, f32[1,384]{1,0:T(1,128)S(1)} %get-tuple-element.168.b_ref, ...), custom_call_target="tpu_custom_call" | custom-call | flops 3758096384 | bytes 6815744 | tf_op jit(solution)/shard_map/pallas_call | solution.py:145
  292.6 7.7 %collective-permute-done.79 = bf16[1024,128]{1,0:T(8,128)(2,1)} collective-permute-done((bf16[1024,128]{1,0:T(8,128)(2,1)}, bf16[1024,128]{1,0:T(8,128)(2,1)}, u32[]{:S(2)}, u32[]{:S(2)}) %collective-permute-start.79) | collective-permute-done | bytes 262176 | tf_op jit(solution)/shard_map/ppermute | solution.py:31
  311.6 4.4 convert_reduce_fusion.2
  319.2 6.9 %fusion.92 = (f32[1024]{0:T(1024)S(1)}, f32[1024]{0:T(1024)S(1)}, f32[1024]{0:T(1024)S(1)}, f32[1024]{0:T(1024)S(1)}, f32[1024,1024]{1,0:T(8,128)S(1)}, /*index=...) fusion(f32[1024]{0:T(1024)S(1)} %get-tuple-element.176, f32[1024]{0:T(1024)S(1)} %get-tuple-element.175, ...), kind=kOutput, calls=%fused_computation.278 | convolution fusion | flops 1092610048 | bytes 29401088 | tf_op jit(solution)/shard_map/dot_general | solution.py:23
  332.0 4.6 fusion.128
  336.6 10.0 %fusion.119 = (bf16[1024,1024]{1,0:T(8,128)(2,1)S(1)}, f32[1024,1024]{1,0:T(8,128)}) fusion(bf16[1024,128]{1,0:T(8,128)(2,1)S(1)} %get-tuple-element.29, bf16[1024,128]{1,0:T(8,128)(2,1)S(1)} %copy-done.10, f32[1024,1024]{1,0:T(8,128)S(1)} %copy-done.23, f32[1024,1024]{1,0:T(8,128)S(1)} %copy-done.22, f32[1024,1024]{1,0:T(8,128)S(1)} %copy-done.24, ...), kind=kOutput, calls=%fused_computation.302 | convolution fusion | flops 276824064 | bytes 36175872 | tf_op jit(solution)/shard_map/dot_general | solution.py:23
  427.0 5.8 collective-permute-done.45
  433.3 11.0 %collective-permute-done.47 = bf16[1024,128]{1,0:T(8,128)(2,1)} collective-permute-done((bf16[1024,128]{1,0:T(8,128)(2,1)}, bf16[1024,128]{1,0:T(8,128)(2,1)}, u32[]{:S(2)}, u32[]{:S(2)}) %collective-permute-start.47) | collective-permute-done | bytes 262176 | tf_op jit(solution)/shard_map/ppermute | solution.py:31
  450.9 9.9 %collective-permute-done.50 = bf16[2,1024,128]{2,1,0:T(8,128)(2,1)S(1)} collective-permute-done((bf16[2,1024,128]{2,1,0:T(8,128)(2,1)S(1)}, bf16[2,1024,128]{2,1,0:T(8,128)(2,1)S(1)}, u32[]{:S(2)}, u32[]{:S(2)}) %collective-permute-start.50) | collective-permute-done | bytes 524320 | tf_op jit(solution)/shard_map/ppermute | solution.py:31
  462.3 9.4 %collective-permute-done.59 = bf16[2,1024,128]{2,1,0:T(8,128)(2,1)S(1)} collective-permute-done((bf16[2,1024,128]{2,1,0:T(8,128)(2,1)S(1)}, bf16[2,1024,128]{2,1,0:T(8,128)(2,1)S(1)}, u32[]{:S(2)}, u32[]{:S(2)}) %collective-permute-start.59) | collective-permute-done | bytes 524320 | tf_op jit(solution)/shard_map/ppermute | solution.py:31
  476.1 5.9 collective-permute-done.72
  486.4 25.0 %collective-permute-done.75 = bf16[256,384]{1,0:T(8,128)(2,1)S(1)} collective-permute-done((bf16[256,384]{1,0:T(8,128)(2,1)S(1)}, bf16[256,384]{1,0:T(8,128)(2,1)S(1)}, u32[]{:S(2)}, u32[]{:S(2)}) %collective-permute-start.75) | collective-permute-done | bytes 196640 | tf_op jit(solution)/shard_map/ppermute | solution.py:31
  517.9 6.1 %rev.88 = bf16[2,2,1,256,384]{3,1,0,4,2:T(2,128)(2,1)} reverse(bf16[2,2,1,256,384]{3,1,0,4,2:T(2,128)(2,1)S(1)} %copy.146), dimensions={1} | reverse | bytes 1572864 | tf_op jit(solution)/shard_map/rev | solution.py:39
  533.3 6.3 %collective-permute-done.97 = bf16[1024,512]{0,1:T(8,128)(2,1)} collective-permute-done((bf16[1024,512]{0,1:T(8,128)(2,1)}, bf16[1024,512]{0,1:T(8,128)(2,1)}, u32[]{:S(2)}, u32[]{:S(2)}) %collective-permute-start.97) | collective-permute-done | bytes 1048608 | tf_op jit(solution)/shard_map/ppermute | solution.py:31
  549.2 16.3 %collective-permute-done.90 = bf16[256,512]{0,1:T(8,128)(2,1)S(1)} collective-permute-done((bf16[256,512]{0,1:T(8,128)(2,1)S(1)}, bf16[256,512]{0,1:T(8,128)(2,1)S(1)}, u32[]{:S(2)}, u32[]{:S(2)}) %collective-permute-start.90) | collective-permute-done | bytes 262176 | tf_op jit(solution)/shard_map/ppermute | solution.py:31
  567.0 9.6 %collective-permute-done.99 = bf16[256,512]{0,1:T(8,128)(2,1)S(1)} collective-permute-done((bf16[256,512]{0,1:T(8,128)(2,1)S(1)}, bf16[256,512]{0,1:T(8,128)(2,1)S(1)}, u32[]{:S(2)}, u32[]{:S(2)}) %collective-permute-start.99) | collective-permute-done | bytes 262176 | tf_op jit(solution)/shard_map/ppermute | solution.py:31
  (598 shorter events, 339.6 us)
Async XLA Ops:
  2.9 43.2 %collective-permute-start.10 = (f32[5,256]{1,0:T(8,128)}, f32[5,256]{1,0:T(8,128)}, u32[]{:S(2)}, u32[]{:S(2)}) collective-permute-start(f32[5,256]{1,0:T(8,128)} %fusion.84), channel_id=1, source_target_pairs={{0,3},{1,2},{2,1},{3,0},{4,7},{5,6},{6,5},{7,4},{8,11},{9,10},{10,... | collective-permute-start | bytes 15368 | tf_op jit(solution)/shard_map/ppermute | solution.py:31
  7.9 40.8 %collective-permute-start.9 = (f32[5,256]{1,0:T(8,128)}, f32[5,256]{1,0:T(8,128)}, u32[]{:S(2)}, u32[]{:S(2)}) collective-permute-start(f32[5,256]{1,0:T(8,128)} %fusion.84), channel_id=1, source_target_pairs={{0,2},{1,3},{2,0},{3,1},{4,6},{5,7},{6,4},{7,5},{8,10},{9,11},{10,... | collective-permute-start | bytes 15368 | tf_op jit(solution)/shard_map/ppermute | solution.py:31
  7.9 43.5 %collective-permute-start.8 = (f32[5,256]{1,0:T(8,128)}, f32[5,256]{1,0:T(8,128)}, u32[]{:S(2)}, u32[]{:S(2)}) collective-permute-start(f32[5,256]{1,0:T(8,128)} %fusion.84), channel_id=1, source_target_pairs={{0,1},{1,0},{2,3},{3,2},{4,5},{5,4},{6,7},{7,6},{8,9},{9,8},{10,11... | collective-permute-start | bytes 15368 | tf_op jit(solution)/shard_map/ppermute | solution.py:31
  14.2 54.5 %collective-permute-start.25 = (bf16[256,384]{1,0:T(8,128)(2,1)S(1)}, bf16[256,384]{1,0:T(8,128)(2,1)S(1)}, u32[]{:S(2)}, u32[]{:S(2)}) collective-permute-start(bf16[256,384]{1,0:T(8,128)(2,1)S(1)} %maximum_select_fusion.4), channel_id=1, source_target_pairs={{0,3},{1,2},{2,1},{3,0},{4,7},{5,6},{6,5},{7,4},{8,11},{9,10},{10,... | collective-permute-start | bytes 589832 | tf_op jit(solution)/shard_map/ppermute | solution.py:31
  18.1 51.7 %collective-permute-start.24 = (bf16[256,384]{1,0:T(8,128)(2,1)S(1)}, bf16[256,384]{1,0:T(8,128)(2,1)}, u32[]{:S(2)}, u32[]{:S(2)}) collective-permute-start(bf16[256,384]{1,0:T(8,128)(2,1)S(1)} %maximum_select_fusion.4), channel_id=1, source_target_pairs={{0,2},{1,3},{2,0},{3,1},{4,6},{5,7},{6,4},{7,5},{8,10},{9,11},{10,... | collective-permute-start | bytes 589832 | tf_op jit(solution)/shard_map/ppermute | solution.py:31
  54.8 35.1 %collective-permute-start.12 = (bf16[256,512]{0,1:T(8,128)(2,1)}, bf16[256,512]{0,1:T(8,128)(2,1)S(1)}, u32[]{:S(2)}, u32[]{:S(2)}) collective-permute-start(bf16[256,512]{0,1:T(8,128)(2,1)} %maximum_select_fusion), channel_id=1, source_target_pairs={{0,2},{1,3},{2,0},{3,1},{4,6},{5,7},{6,4},{7,5},{8,10},{9,11},{10,... | collective-permute-start | bytes 786440 | tf_op jit(solution)/shard_map/ppermute | solution.py:31
  69.8 33.1 %collective-permute-start = (bf16[2,1024,128]{2,1,0:T(8,128)(2,1)}, bf16[2,1024,128]{2,1,0:T(8,128)(2,1)S(1)}, u32[]{:S(2)}, u32[]{:S(2)}) collective-permute-start(bf16[2,1024,128]{2,1,0:T(8,128)(2,1)} %broadcast_select_fusion.16), channel_id=1, source_target_pairs={{0,4},{4,0},{1,5},{5,1},{2,6},{6,2},{3,7},{7,3},{8,12},{12,8},{9,1... | collective-permute-start | bytes 1572872 | tf_op jit(solution)/shard_map/ppermute | solution.py:31
  118.9 82.7 %collective-permute-start.40 = (bf16[1024,128]{1,0:T(8,128)(2,1)S(1)}, bf16[1024,128]{1,0:T(8,128)(2,1)S(1)}, u32[]{:S(2)}, u32[]{:S(2)}) collective-permute-start(bf16[1024,128]{1,0:T(8,128)(2,1)S(1)} %pad_maximum_fusion.12.wd_ref), channel_id=1, source_target_pairs={{0,16},{8,24},{16,0},{24,8},{1,17},{9,25},{17,1},{25,9},{2,18},{10... | collective-permute-start | bytes 786440 | tf_op jit(solution)/shard_map/ppermute | solution.py:31
  125.5 58.4 %collective-permute-start.38 = (bf16[1024,128]{1,0:T(8,128)(2,1)S(1)}, bf16[1024,128]{1,0:T(8,128)(2,1)S(1)}, u32[]{:S(2)}, u32[]{:S(2)}) collective-permute-start(bf16[1024,128]{1,0:T(8,128)(2,1)S(1)} %pad_maximum_fusion.12.wd_ref), channel_id=1, source_target_pairs={{0,8},{8,0},{16,24},{24,16},{1,9},{9,1},{17,25},{25,17},{2,10},{10... | collective-permute-start | bytes 786440 | tf_op jit(solution)/shard_map/ppermute | solution.py:31
  127.2 74.6 %collective-permute-start.39 = (bf16[1024,384]{1,0:T(8,128)(2,1)S(1)}, bf16[1024,384]{1,0:T(8,128)(2,1)S(1)}, u32[]{:S(2)}, u32[]{:S(2)}) collective-permute-start(bf16[1024,384]{1,0:T(8,128)(2,1)S(1)} %pad_maximum_fusion.6.wq_ref), channel_id=1, source_target_pairs={{0,16},{8,24},{16,0},{24,8},{1,17},{9,25},{17,1},{25,9},{2,18},{10... | collective-permute-start | bytes 2359304 | tf_op jit(solution)/shard_map/ppermute | solution.py:31
  163.7 71.2 %collective-permute-start.19 = (bf16[1024,512]{0,1:T(8,128)(2,1)}, bf16[1024,512]{0,1:T(8,128)(2,1)}, u32[]{:S(2)}, u32[]{:S(2)}) collective-permute-start(bf16[1024,512]{0,1:T(8,128)(2,1)} %pad_maximum_fusion), channel_id=1, source_target_pairs={{0,16},{8,24},{16,0},{24,8},{1,17},{9,25},{17,1},{25,9},{2,18},{10... | collective-permute-start | bytes 3145736 | tf_op jit(solution)/shard_map/ppermute | solution.py:31
  183.9 48.3 %collective-permute-start.17 = (bf16[1024,512]{0,1:T(8,128)(2,1)}, bf16[1024,512]{0,1:T(8,128)(2,1)}, u32[]{:S(2)}, u32[]{:S(2)}) collective-permute-start(bf16[1024,512]{0,1:T(8,128)(2,1)} %pad_maximum_fusion), channel_id=1, source_target_pairs={{0,8},{8,0},{16,24},{24,16},{1,9},{9,1},{17,25},{25,17},{2,10},{10... | collective-permute-start | bytes 3145736 | tf_op jit(solution)/shard_map/ppermute | solution.py:31
  184.0 64.2 %collective-permute-start.20 = (bf16[1024,512]{0,1:T(8,128)(2,1)}, bf16[1024,512]{0,1:T(8,128)(2,1)}, u32[]{:S(2)}, u32[]{:S(2)}) collective-permute-start(bf16[1024,512]{0,1:T(8,128)(2,1)} %pad_maximum_fusion.1), channel_id=1, source_target_pairs={{0,16},{8,24},{16,0},{24,8},{1,17},{9,25},{17,1},{25,9},{2,18},{10... | collective-permute-start | bytes 3145736 | tf_op jit(solution)/shard_map/ppermute | solution.py:31
  201.6 33.7 %collective-permute-start.18 = (bf16[1024,512]{0,1:T(8,128)(2,1)}, bf16[1024,512]{0,1:T(8,128)(2,1)}, u32[]{:S(2)}, u32[]{:S(2)}) collective-permute-start(bf16[1024,512]{0,1:T(8,128)(2,1)} %pad_maximum_fusion.1), channel_id=1, source_target_pairs={{0,8},{8,0},{16,24},{24,16},{1,9},{9,1},{17,25},{25,17},{2,10},{10... | collective-permute-start | bytes 3145736 | tf_op jit(solution)/shard_map/ppermute | solution.py:31
  201.8 67.3 %collective-permute-start.42 = (bf16[1024,128]{1,0:T(8,128)(2,1)S(1)}, bf16[1024,128]{1,0:T(8,128)(2,1)S(1)}, u32[]{:S(2)}, u32[]{:S(2)}) collective-permute-start(bf16[1024,128]{1,0:T(8,128)(2,1)S(1)} %collective-permute-done.40.wd_ref), channel_id=1, source_target_pairs={{0,8},{8,0},{16,24},{24,16},{1,9},{9,1},{17,25},{25,17},{2,10},{10... | collective-permute-start | bytes 786440 | tf_op jit(solution)/shard_map/ppermute | solution.py:31
  232.2 36.9 %collective-permute-start.41 = (bf16[1024,384]{1,0:T(8,128)(2,1)S(1)}, bf16[1024,384]{1,0:T(8,128)(2,1)S(1)}, u32[]{:S(2)}, u32[]{:S(2)}) collective-permute-start(bf16[1024,384]{1,0:T(8,128)(2,1)S(1)} %collective-permute-done.39.wq_ref), channel_id=1, source_target_pairs={{0,8},{8,0},{16,24},{24,16},{1,9},{9,1},{17,25},{25,17},{2,10},{10... | collective-permute-start | bytes 2359304 | tf_op jit(solution)/shard_map/ppermute | solution.py:31
  234.9 57.7 %collective-permute-start.77 = (bf16[1024,128]{1,0:T(8,128)(2,1)}, bf16[1024,128]{1,0:T(8,128)(2,1)}, u32[]{:S(2)}, u32[]{:S(2)}) collective-permute-start(bf16[1024,128]{1,0:T(8,128)(2,1)} %convolution_convert_fusion.7), channel_id=1, source_target_pairs={{0,8},{8,0},{16,24},{24,16},{1,9},{9,1},{17,25},{25,17},{2,10},{10... | collective-permute-start | bytes 786440 | tf_op jit(solution)/shard_map/ppermute | solution.py:31
  235.3 73.2 %collective-permute-start.21 = (bf16[1024,512]{0,1:T(8,128)(2,1)}, bf16[1024,512]{0,1:T(8,128)(2,1)}, u32[]{:S(2)}, u32[]{:S(2)}) collective-permute-start(bf16[1024,512]{0,1:T(8,128)(2,1)} %collective-permute-done.19), channel_id=1, source_target_pairs={{0,8},{8,0},{16,24},{24,16},{1,9},{9,1},{17,25},{25,17},{2,10},{10... | collective-permute-start | bytes 3145736 | tf_op jit(solution)/shard_map/ppermute | solution.py:31
  248.2 63.3 %collective-permute-start.22 = (bf16[1024,512]{0,1:T(8,128)(2,1)}, bf16[1024,512]{0,1:T(8,128)(2,1)}, u32[]{:S(2)}, u32[]{:S(2)}) collective-permute-start(bf16[1024,512]{0,1:T(8,128)(2,1)} %collective-permute-done.20), channel_id=1, source_target_pairs={{0,8},{8,0},{16,24},{24,16},{1,9},{9,1},{17,25},{25,17},{2,10},{10... | collective-permute-start | bytes 3145736 | tf_op jit(solution)/shard_map/ppermute | solution.py:31
  282.0 133.5 %collective-permute-start.69 = (bf16[1024,384]{1,0:T(8,128)(2,1)}, bf16[1024,384]{1,0:T(8,128)(2,1)}, u32[]{:S(2)}, u32[]{:S(2)}) collective-permute-start(bf16[1024,384]{1,0:T(8,128)(2,1)} %convolution_convert_fusion.4), channel_id=1, source_target_pairs={{0,8},{8,0},{16,24},{24,16},{1,9},{9,1},{17,25},{25,17},{2,10},{10... | collective-permute-start | bytes 2359304 | tf_op jit(solution)/shard_map/ppermute | solution.py:31
  304.3 46.5 %collective-permute-start.82 = (bf16[256,128]{1,0:T(8,128)(2,1)}, bf16[256,128]{1,0:T(8,128)(2,1)S(1)}, u32[]{:S(2)}, u32[]{:S(2)}) collective-permute-start(bf16[256,128]{1,0:T(8,128)(2,1)} %get-tuple-element.130), channel_id=1, source_target_pairs={{0,3},{1,2},{2,1},{3,0},{4,7},{5,6},{6,5},{7,4},{8,11},{9,10},{10,... | collective-permute-start | bytes 196616 | tf_op jit(solution)/shard_map/ppermute | solution.py:31
  307.3 43.7 %collective-permute-start.81 = (bf16[256,128]{1,0:T(8,128)(2,1)}, bf16[256,128]{1,0:T(8,128)(2,1)}, u32[]{:S(2)}, u32[]{:S(2)}) collective-permute-start(bf16[256,128]{1,0:T(8,128)(2,1)} %get-tuple-element.131), channel_id=1, source_target_pairs={{0,2},{1,3},{2,0},{3,1},{4,6},{5,7},{6,4},{7,5},{8,10},{9,11},{10,... | collective-permute-start | bytes 196616 | tf_op jit(solution)/shard_map/ppermute | solution.py:31
  308.5 44.0 %collective-permute-start.80 = (bf16[256,128]{1,0:T(8,128)(2,1)}, bf16[256,128]{1,0:T(8,128)(2,1)}, u32[]{:S(2)}, u32[]{:S(2)}) collective-permute-start(bf16[256,128]{1,0:T(8,128)(2,1)} %get-tuple-element.129), channel_id=1, source_target_pairs={{0,1},{1,0},{2,3},{3,2},{4,5},{5,4},{6,7},{7,6},{8,9},{9,8},{10,11... | collective-permute-start | bytes 196616 | tf_op jit(solution)/shard_map/ppermute | solution.py:31
  432.8 92.0 %collective-permute-start.86 = (bf16[1024,512]{0,1:T(8,128)(2,1)}, bf16[1024,512]{0,1:T(8,128)(2,1)}, u32[]{:S(2)}, u32[]{:S(2)}) collective-permute-start(bf16[1024,512]{0,1:T(8,128)(2,1)} %convolution_convert_fusion.3), channel_id=1, source_target_pairs={{0,8},{8,0},{16,24},{24,16},{1,9},{9,1},{17,25},{25,17},{2,10},{10... | collective-permute-start | bytes 3145736 | tf_op jit(solution)/shard_map/ppermute | solution.py:31
  432.8 39.2 %collective-permute-start.87 = (bf16[1024,512]{0,1:T(8,128)(2,1)}, bf16[1024,512]{0,1:T(8,128)(2,1)S(1)}, u32[]{:S(2)}, u32[]{:S(2)}) collective-permute-start(bf16[1024,512]{0,1:T(8,128)(2,1)} %convolution_convert_fusion.2), channel_id=1, source_target_pairs={{0,8},{8,0},{16,24},{24,16},{1,9},{9,1},{17,25},{25,17},{2,10},{10... | collective-permute-start | bytes 3145736 | tf_op jit(solution)/shard_map/ppermute | solution.py:31
  444.3 42.2 %collective-permute-start.96 = (bf16[1024,512]{0,1:T(8,128)(2,1)}, bf16[1024,512]{0,1:T(8,128)(2,1)S(1)}, u32[]{:S(2)}, u32[]{:S(2)}) collective-permute-start(bf16[1024,512]{0,1:T(8,128)(2,1)} %convolution_convert_fusion), channel_id=1, source_target_pairs={{0,8},{8,0},{16,24},{24,16},{1,9},{9,1},{17,25},{25,17},{2,10},{10... | collective-permute-start | bytes 3145736 | tf_op jit(solution)/shard_map/ppermute | solution.py:31
  476.1 57.2 %collective-permute-start.95 = (bf16[1024,512]{0,1:T(8,128)(2,1)}, bf16[1024,512]{0,1:T(8,128)(2,1)}, u32[]{:S(2)}, u32[]{:S(2)}) collective-permute-start(bf16[1024,512]{0,1:T(8,128)(2,1)} %convolution_convert_fusion.1), channel_id=1, source_target_pairs={{0,8},{8,0},{16,24},{24,16},{1,9},{9,1},{17,25},{25,17},{2,10},{10... | collective-permute-start | bytes 3145736 | tf_op jit(solution)/shard_map/ppermute | solution.py:31
  482.0 42.8 %collective-permute-start.88 = (bf16[1024,512]{0,1:T(8,128)(2,1)}, bf16[1024,512]{0,1:T(8,128)(2,1)}, u32[]{:S(2)}, u32[]{:S(2)}) collective-permute-start(bf16[1024,512]{0,1:T(8,128)(2,1)} %add_convert_fusion.3), channel_id=1, source_target_pairs={{0,16},{8,24},{16,0},{24,8},{1,17},{9,25},{17,1},{25,9},{2,18},{10... | collective-permute-start | bytes 3145736 | tf_op jit(solution)/shard_map/ppermute | solution.py:31
  531.6 33.9 %collective-permute-start.90 = (bf16[256,512]{0,1:T(8,128)(2,1)S(1)}, bf16[256,512]{0,1:T(8,128)(2,1)S(1)}, u32[]{:S(2)}, u32[]{:S(2)}) collective-permute-start(bf16[256,512]{0,1:T(8,128)(2,1)S(1)} %get-tuple-element.105), channel_id=1, source_target_pairs={{0,2},{1,3},{2,0},{3,1},{4,6},{5,7},{6,4},{7,5},{8,10},{9,11},{10,... | collective-permute-start | bytes 786440 | tf_op jit(solution)/shard_map/ppermute | solution.py:31
  531.6 33.9 %collective-permute-start.89 = (bf16[256,512]{0,1:T(8,128)(2,1)S(1)}, bf16[256,512]{0,1:T(8,128)(2,1)S(1)}, u32[]{:S(2)}, u32[]{:S(2)}) collective-permute-start(bf16[256,512]{0,1:T(8,128)(2,1)S(1)} %get-tuple-element.103), channel_id=1, source_target_pairs={{0,1},{1,0},{2,3},{3,2},{4,5},{5,4},{6,7},{7,6},{8,9},{9,8},{10,11... | collective-permute-start | bytes 786440 | tf_op jit(solution)/shard_map/ppermute | solution.py:31
  545.3 31.3 %collective-permute-start.99 = (bf16[256,512]{0,1:T(8,128)(2,1)S(1)}, bf16[256,512]{0,1:T(8,128)(2,1)S(1)}, u32[]{:S(2)}, u32[]{:S(2)}) collective-permute-start(bf16[256,512]{0,1:T(8,128)(2,1)S(1)} %get-tuple-element.102), channel_id=1, source_target_pairs={{0,2},{1,3},{2,0},{3,1},{4,6},{5,7},{6,4},{7,5},{8,10},{9,11},{10,... | collective-permute-start | bytes 786440 | tf_op jit(solution)/shard_map/ppermute | solution.py:31
  545.3 31.3 %collective-permute-start.98 = (bf16[256,512]{0,1:T(8,128)(2,1)S(1)}, bf16[256,512]{0,1:T(8,128)(2,1)S(1)}, u32[]{:S(2)}, u32[]{:S(2)}) collective-permute-start(bf16[256,512]{0,1:T(8,128)(2,1)S(1)} %get-tuple-element.100), channel_id=1, source_target_pairs={{0,1},{1,0},{2,3},{3,2},{4,5},{5,4},{6,7},{7,6},{8,9},{9,8},{10,11... | collective-permute-start | bytes 786440 | tf_op jit(solution)/shard_map/ppermute | solution.py:31
  (168 other events, 2746.3 us)
